TPU v7x, 256 devices: a whole 4x4x8 slice. The times are simulated.
256 devices in a mesh: section: 8 (over z), ep: 32 (over y, x, core).
Axes of the slice: x: 4, y: 4, z: 8, core: 2. Of those that a mesh axis runs over, the one named last changes fastest.
Arguments:
- arriving: bfloat16 [8, 2048, 3072], P('section', 'ep'), may hold values from -6 to 6
- top_grad: bfloat16 [1, 2048, 3072], P(None, 'ep'), may hold values from -6 to 6
- expert_ids: int32 [8, 2, 2048, 2], P('section'), may hold values from 0 to 3, all different within a row; in each aligned block of 64 rows (0 to 63, 64 to 127, ..., all dimensions but the last counted through in order) at most 36 rows name the same one
- first_share: float32 [8, 2, 2048], P('section', None, 'ep'), may hold values from 0.5 to 0.95
- out_gap: bfloat16 [8, 2, 2048, 3072], P('section', None, 'ep'), may hold values from -6 to 6
- router_weight: float32 [8, 4, 3072], P('section'), may hold values from -0.75 to 0.75
- down_weight: bfloat16 [8, 32768, 3072], P('section', 'ep'), may hold values from -0.109375 to 0.109375
Outputs:
- departing: bfloat16 [8, 2, 2048, 3072], P('section', None, 'ep')
- hidden_grad: bfloat16 [8, 2, 36864, 1024], P('section', None, 'ep')
Inputs may be any that keep to these rules, and one draw needn't show every extreme that they name: `expert_ids`: A token's two ids differ; within one step each device's 64 tokens name any one expert at most 36 times.
All inputs are finite; a program needn't handle non-finite values.
Results may differ from a plain program's by a relative error of at most 0.0054.
Values may be sent and summed in bfloat16 or wider, within the bound.
No kernel may reach another device: no remote copies, remote signals or barrier semaphores. Data moves between devices by JAX's collectives and lax.ppermute only.
A program may use at most 128 MiB of HBM per device.

v0:
```python
import functools

import jax
import jax.numpy as jnp
import numpy as np
from jax import lax
from jax.experimental import pallas as pl
from jax.experimental.pallas import tpu as pltpu
from jax.sharding import PartitionSpec as P

TICKS = 2
CAP = 36
XS, YS, CORES = 4, 4, 2
EP = XS * YS * CORES
TOKENS = 64
D = 3072
HID = 1024
MAXP = EP * CAP
BLOCK = YS * CAP
HEAD = 80
DYS = (0, 1, 3, 2)
GROUP = CORES * BLOCK
NEAR = 3 * GROUP
OWN = 32
STEP = 128
PLACED = 384
ORDER = ((0, 0), (1, 0), (3, 0), (0, 1), (1, 1), (3, 1), (2, 0), (2, 1))
VMEM = pl.BlockSpec(memory_space=pltpu.VMEM)
ANY = pl.BlockSpec(memory_space=pl.ANY)
HBM = pl.BlockSpec(memory_space=pltpu.HBM)
CHEAP = pl.CostEstimate(flops=1024, bytes_accessed=1024, transcendentals=0)
SOME = pl.CostEstimate(flops=1200 << 20, bytes_accessed=1024, transcendentals=0)
NT = (((1,), (1,)), ((), ()))


def hop(shard, dy=0, dx=0, dc=0):
    pairs = []
    for y in range(YS):
        for x in range(XS):
            for c in range(CORES):
                to = (((y + dy) % YS) * XS + (x + (dx, -dx)[c]) % XS) * CORES + (c + dc) % CORES
                pairs.append(((y * XS + x) * CORES + c, to))
    return lax.ppermute(shard, "ep", pairs)


def down(shard):
    n = lax.axis_size("section")
    return lax.ppermute(shard, "section", [(i, i - 1) for i in range(1, n)])


def front_kernel(moment, count, ids_hbm, share_hbm, router_hbm, gap_hbm, *refs):
    grads, outs = refs[:count], refs[-15:-8]
    ids_ref, share_ref, router_ref, gap_ref, grads_ref, parts_ref, departing_ref, sems = refs[-8:]
    pairs = [(ids_hbm.at[moment], ids_ref), (share_hbm, share_ref)]
    pairs += [(grads[i], grads_ref.at[i]) for i in range(count)]
    pairs += [(gap_hbm.at[moment], gap_ref), (router_hbm, router_ref)]
    loads = [pltpu.make_async_copy(source, to, sems.at[i]) for i, (source, to) in enumerate(pairs)]
    for load in loads:
        load.start()
    for load in loads[: 2 + count]:
        load.wait()
    me = lax.axis_index("ep")
    both = ids_ref[:, pl.ds(pl.multiple_of((me // 2) * 128, 128), 128)].astype(jnp.float32)
    own = jnp.where(me % 2 == 0, both[:, :TOKENS], both[:, TOKENS:])
    first, second = own[0:1], own[1:2]
    share = share_ref[moment : moment + 1, :]
    gradient = grads_ref[0]
    if count == 2:
        last = lax.axis_index("section") == lax.axis_size("section") - 1
        gradient = jnp.where(last, gradient, grads_ref[1])

    my_y = (me // (XS * CORES)).astype(jnp.float32)
    experts = lax.broadcasted_iota(jnp.int32, (8, TOKENS), 0).astype(jnp.float32)
    is_first, is_second = experts == first, experts == second
    chosen = (is_first | is_second).astype(jnp.float32).astype(jnp.bfloat16)
    rows = lax.broadcasted_iota(jnp.int32, (TOKENS, TOKENS), 0)
    columns = lax.broadcasted_iota(jnp.int32, (TOKENS, TOKENS), 1)
    before = (rows < columns).astype(jnp.float32).astype(jnp.bfloat16)
    ranks = jnp.dot(chosen, before, preferred_element_type=jnp.float32)

    def placed(expert, mask):
        relative = expert - my_y
        relative = jnp.where(relative < 0, relative + YS, relative)
        return relative * CAP + jnp.sum(jnp.where(mask, ranks, 0.0), 0, keepdims=True)

    place_1, place_2 = placed(first, is_first), placed(second, is_second)
    slots = lax.broadcasted_iota(jnp.int32, (CAP, TOKENS), 0).astype(jnp.float32)
    stores = []
    for j in range(YS):
        one, two = slots + j * CAP == place_1, slots + j * CAP == place_2
        weight = jnp.sum(jnp.where(one, share, 0.0) + jnp.where(two, 1.0 - share, 0.0), 1, keepdims=True)
        placing = (one | two).astype(jnp.float32).astype(jnp.bfloat16)
        gathered = jnp.dot(placing, gradient, preferred_element_type=jnp.float32)
        parts_ref[j] = (gathered * weight).astype(jnp.bfloat16)
        stores.append(pltpu.make_async_copy(parts_ref.at[j], outs[j], sems.at[4 + count + j]))
        stores[j].start()
    stores.append(pltpu.make_async_copy(parts_ref.at[0, pl.ds(0, OWN)], outs[YS], sems.at[4 + count + YS]))
    stores[YS].start()

    def upright(row):
        return jnp.sum(jnp.where(rows == columns, row, 0.0), 1, keepdims=True)

    for load in loads[2 + count :]:
        load.wait()
    first, second, share = upright(first), upright(second), upright(share)
    gradient = gradient.astype(jnp.float32)
    gap_dot = jnp.sum(gradient * gap_ref[...].astype(jnp.float32), 1, keepdims=True)
    logit_grad = share * (1.0 - share) * gap_dot
    term = jnp.zeros((TOKENS, D), jnp.float32)
    for e in range(YS):
        sign = jnp.where(first == e, 1.0, 0.0) - jnp.where(second == e, 1.0, 0.0)
        term = term + (logit_grad * sign) * router_ref[e : e + 1, :]
    departing_ref[...] = (gradient + term).astype(jnp.bfloat16)
    for to in (outs[YS + 1].at[moment], outs[YS + 2]):
        stores.append(pltpu.make_async_copy(departing_ref, to, sems.at[4 + count + len(stores)]))
        stores[-1].start()
    for store in stores:
        store.wait()


def front(moment, ids, share, router_rows, gap, grads, departs):
    more = [] if departs is None else [departs]
    count = len(grads)
    return pl.pallas_call(
        functools.partial(front_kernel, moment, count),
        out_shape=[jax.ShapeDtypeStruct((CAP, D), jnp.bfloat16)] * YS
        + [
            jax.ShapeDtypeStruct((OWN, D), jnp.bfloat16),
            jax.ShapeDtypeStruct((TICKS, TOKENS, D), jnp.bfloat16),
            jax.ShapeDtypeStruct((TOKENS, D), jnp.bfloat16),
        ],
        in_specs=[HBM] * (4 + count + len(more)),
        out_specs=[HBM] * (YS + 3),
        scratch_shapes=[
            pltpu.VMEM((2, EP * TOKENS), jnp.int32),
            pltpu.VMEM((TICKS, TOKENS), jnp.float32),
            pltpu.VMEM((YS, D), jnp.float32),
            pltpu.VMEM((TOKENS, D), jnp.bfloat16),
            pltpu.VMEM((count, TOKENS, D), jnp.bfloat16),
            pltpu.VMEM((YS, CAP, D), jnp.bfloat16),
            pltpu.VMEM((TOKENS, D), jnp.bfloat16),
            pltpu.SemaphoreType.DMA((4 + count + YS + 3,)),
        ],
        input_output_aliases={4 + count: YS + 1} if more else {},
        compiler_params=pltpu.CompilerParams(vmem_limit_bytes=60 << 20),
        cost_estimate=CHEAP,
        name="front",
    )(ids, share, router_rows, gap, *grads, *more)


def each(count, unrolled, body):
    if unrolled or count == 1:
        for k in range(count):
            body(k)
    else:
        pl.loop(0, count)(body)


def multiply(pieces, rows_ref, down_ref, product_ref, unrolled):
    begin = 0
    for piece in pieces:
        rows_ref[pl.ds(begin, piece.shape[0]), :] = piece[...]
        begin += piece.shape[0]

    def group(k):
        part = pl.ds(pl.multiple_of(k * GROUP, GROUP), GROUP)
        product = lax.dot_general(rows_ref[part, :], down_ref[...], NT, preferred_element_type=jnp.float32)
        product_ref[part, :] = product.astype(jnp.bfloat16)

    each(begin // GROUP, unrolled, group)


def plan_kernel(ids_ref, table_ref, *outs):
    me = lax.axis_index("ep")
    my_y, my_x, my_c = me // (XS * CORES), (me // CORES) % XS, me % CORES
    table = table_ref[...]
    source_c = (my_c - table[2:3]) & (CORES - 1)
    source_x = jnp.where(source_c == 0, my_x - table[1:2], my_x + table[1:2]) & (XS - 1)
    source = ((my_y - table[0:1]) & (YS - 1)) * (XS * CORES) + source_x * CORES + source_c
    slot = table[3:4].astype(jnp.float32)
    device = lax.broadcasted_iota(jnp.int32, (EP, MAXP), 0)
    ahead = (device < source).astype(jnp.float32).astype(jnp.bfloat16)
    itself = (device == source).astype(jnp.float32).astype(jnp.bfloat16)
    owner = lax.broadcasted_iota(jnp.int32, (EP, EP * TOKENS), 1) // TOKENS
    owned = (owner == lax.broadcasted_iota(jnp.int32, (EP, EP * TOKENS), 0)).astype(jnp.float32).astype(jnp.bfloat16)
    for moment in range(TICKS):
        named = (ids_ref[moment] == my_y).astype(jnp.float32)
        named = jnp.broadcast_to(named[0:1] + named[1:2], (8, EP * TOKENS)).astype(jnp.bfloat16)
        counts = lax.dot_general(named, owned, NT, preferred_element_type=jnp.float32).astype(jnp.bfloat16)
        offset = jnp.dot(counts, ahead, preferred_element_type=jnp.float32)[0:1]
        amount = jnp.dot(counts, itself, preferred_element_type=jnp.float32)[0:1]
        target = jnp.where(slot < amount, offset + slot, -1.0).astype(jnp.int32)

        for i, part in enumerate((target[:, :NEAR], target[:, NEAR:])):

            @pl.loop(0, MAXP // STEP)
            def _(k, out=outs[2 * moment + i], part=part):
                at = pl.multiple_of(k * STEP, STEP)
                here = lax.broadcasted_iota(jnp.int32, (STEP, part.shape[1]), 0) + at
                out[pl.ds(at, STEP), :] = (here == part).astype(jnp.float32).astype(jnp.bfloat16)


def plan(ids):
    columns = [(dy, dx, dc, slot) for dx, dc in ORDER for dy in DYS for slot in range(CAP)]
    table = np.zeros((8, MAXP), np.int32)
    table[:4] = np.array(columns, np.int32).T
    return pl.pallas_call(
        plan_kernel,
        out_shape=[jax.ShapeDtypeStruct((MAXP, n), jnp.bfloat16) for n in (NEAR, GROUP)] * TICKS,
        in_specs=[VMEM] * 2,
        out_specs=[VMEM] * (2 * TICKS),
        compiler_params=pltpu.CompilerParams(vmem_limit_bytes=16 << 20),
        cost_estimate=CHEAP,
        name="plan",
    )(ids, jnp.asarray(table))


def near_kernel(count, unrolled, placing_ref, down_ref, *refs):
    out_ref, rows_ref, product_ref = refs[count:]
    multiply(refs[:count], rows_ref, down_ref, product_ref, unrolled)

    def place(k):
        part = pl.ds(pl.multiple_of(k * PLACED, PLACED), PLACED)
        placed = jnp.dot(placing_ref[part, :], product_ref[...], preferred_element_type=jnp.float32)
        out_ref[part, :] = placed.astype(jnp.bfloat16)

    each(MAXP // PLACED, unrolled, place)


def near_product(placing, pieces, down_rows, unrolled):
    return pl.pallas_call(
        functools.partial(near_kernel, len(pieces), unrolled),
        out_shape=jax.ShapeDtypeStruct((MAXP, HID), jnp.bfloat16),
        in_specs=[VMEM] * (2 + len(pieces)),
        out_specs=VMEM,
        scratch_shapes=[
            pltpu.VMEM((NEAR, D), jnp.bfloat16),
            pltpu.VMEM((NEAR, HID), jnp.bfloat16),
        ],
        compiler_params=pltpu.CompilerParams(vmem_limit_bytes=24 << 20),
        cost_estimate=CHEAP,
        name="near_product",
    )(placing, down_rows, *pieces)


def far_kernel(moment, count, placing_ref, down_ref, near_ref, *refs):
    out_ref, rows_ref, product_ref, placed_ref, sems = refs[-5:]
    multiply(refs[:count], rows_ref, down_ref, product_ref, True)
    stores = []
    for k in range(MAXP // PLACED):
        part = pl.ds(k * PLACED, PLACED)
        placed = jnp.dot(placing_ref[part, :], product_ref[...], preferred_element_type=jnp.float32)
        placed_ref[part, :] = (placed + near_ref[part, :].astype(jnp.float32)).astype(jnp.bfloat16)
        stores.append(pltpu.make_async_copy(placed_ref.at[part], out_ref.at[moment, part], sems.at[k]))
        stores[k].start()
    for store in stores:
        store.wait()


def far_product(moment, placing, pieces, near, down_rows, hidden):
    more = [] if hidden is None else [hidden]
    return pl.pallas_call(
        functools.partial(far_kernel, moment, len(pieces)),
        out_shape=jax.ShapeDtypeStruct((TICKS, MAXP, HID), jnp.bfloat16),
        in_specs=[VMEM] * (3 + len(pieces)) + [ANY] * len(more),
        out_specs=ANY,
        scratch_shapes=[
            pltpu.VMEM((GROUP, D), jnp.bfloat16),
            pltpu.VMEM((GROUP, HID), jnp.bfloat16),
            pltpu.VMEM((MAXP, HID), jnp.bfloat16),
            pltpu.SemaphoreType.DMA((MAXP // PLACED,)),
        ],
        input_output_aliases={3 + len(pieces): 0} if more else {},
        compiler_params=pltpu.CompilerParams(vmem_limit_bytes=24 << 20),
        cost_estimate=SOME,
        name="far_product",
    )(placing, down_rows, near, *pieces, *more)


def spread(parts):
    return {j: hop(parts[j], dy=j) for j in (1, 3, 2)}


def joined(own, came):
    return jnp.concatenate([own, came[1], came[3], came[2]], 0)


def swapped(tree):
    return jax.tree.map(lambda p: hop(p, dc=1), tree)


def local(arriving, top_grad, expert_ids, first_share, out_gap, router_weight, down_weight):
    tie = lax.optimization_barrier
    ids = jnp.swapaxes(expert_ids[0], 1, 2)
    share, gap, router_rows, down_rows = first_share[0], out_gap[0], router_weight[0], down_weight[0]

    *parts0, head0, departs, departing = front(0, ids, share, router_rows, gap, [arriving[0]], None)
    grads = [top_grad[0], down(departing)]
    *parts1, _, departs, _ = front(1, ids, share, router_rows, gap, grads, departs)
    first0 = hop(head0, dx=1)
    own0, came0, first0, parts1, departs = tie((parts0[0], spread(parts0), first0, parts1, departs))

    block0 = joined(own0, came0)
    near0 = {1: [first0, hop(block0[OWN:], dx=1)], 3: [hop(block0, dx=3)]}
    placing = plan(ids)
    own1, came1, block0, near0, placing = tie((parts1[0], spread(parts1), block0, near0, placing))

    block1 = joined(own1, came1)
    far0 = hop(near0[3][0], dx=3)
    near1 = {dx: [hop(block1, dx=dx)] for dx in (1, 3)}
    pieces = [block0, *near0[1], *near0[3]]
    product0 = near_product(placing[0], [*pieces, swapped(jnp.concatenate(pieces))], down_rows, False)
    far0, product0 = tie((far0, product0))
    hidden = far_product(0, placing[1], [far0, *swapped([far0[:HEAD], far0[HEAD:]])], product0, down_rows, None)
    block1, near1, hidden = tie((block1, near1, hidden))

    far1 = hop(near1[1][0], dx=1)
    pieces = [block1, *near1[1], *near1[3]]
    product1 = near_product(placing[2], [*pieces, swapped(jnp.concatenate(pieces))], down_rows, True)
    far1, product1 = tie((far1, product1))

    hidden = far_product(1, placing[3], [far1, swapped(far1)], product1, down_rows, hidden)
    return departs[None], hidden[None]


def solution(mesh):
    placed = (
        P("section", "ep", None),
        P(None, "ep", None),
        P("section", None, None, None),
        P("section", None, "ep"),
        P("section", None, "ep", None),
        P("section", None, None),
        P("section", "ep", None),
    )
    return jax.shard_map(
        local,
        mesh=mesh,
        in_specs=placed,
        out_specs=(P("section", None, "ep", None), P("section", None, "ep", None)),
        check_vma=False,
    )
```

profile of v0, /device:TPU:249, one launch (start us, length us, event | category | flops | bytes accessed | tf_op | source)
XLA Modules:
  0.0 98.1 jit_solution(7269952893699779635)
XLA Ops:
  0.6 3.1 %front.2 = (bf16[36,3072]{1,0:T(8,128)(2,1)}, bf16[36,3072]{1,0:T(8,128)(2,1)}, bf16[36,3072]{1,0:T(8,128)(2,1)}, bf16[36,3072]{1,0:T(8,128)(2,1)}, bf16[32,3072...) custom-call(s32[2,2,2048]{2,1,0:T(2,128)} %bitcast.15, f32[2,64]{1,0:T(2,128)} %bitcast.26, ...), custom_call_target="tpu_custom_call" | custom-call | flops 1024 | bytes 1024 | tf_op jit(solution)/shard_map/front/pallas_call | solution.py:124
  3.7 2.7 %collective-permute-start.4 = (bf16[64,3072]{1,0:T(8,128)(2,1)}, bf16[64,3072]{1,0:T(8,128)(2,1)S(1)}, u32[]{:S(2)}, u32[]{:S(2)}) collective-permute-start(bf16[64,3072]{1,0:T(8,128)(2,1)} %get-tuple-element.53), channel_id=1, source_target_pairs={{32,0},{64,32},{96,64},{128,96},{160,128},{192,160},{224,192},{33,... | collective-permute-start | bytes 1179656 | tf_op jit(solution)/shard_map/ppermute | solution.py:48
  6.5 2.2 %collective-permute-start.1 = (bf16[36,3072]{1,0:T(8,128)(2,1)}, bf16[36,3072]{1,0:T(8,128)(2,1)S(1)}, u32[]{:S(2)}, u32[]{:S(2)}) collective-permute-start(bf16[36,3072]{1,0:T(8,128)(2,1)} %get-tuple-element.50), channel_id=1, source_target_pairs={{0,16},{1,17},{2,18},{3,19},{4,20},{5,21},{6,22},{7,23},{8,24},{9,... | collective-permute-start | bytes 663560 | tf_op jit(solution)/shard_map/ppermute | solution.py:43
  8.7 2.5 %collective-permute-start.3 = (bf16[32,3072]{1,0:T(8,128)(2,1)}, bf16[32,3072]{1,0:T(8,128)(2,1)S(1)}, u32[]{:S(2)}, u32[]{:S(2)}) collective-permute-start(bf16[32,3072]{1,0:T(8,128)(2,1)} %get-tuple-element.52), channel_id=1, source_target_pairs={{0,2},{1,7},{2,4},{3,1},{4,6},{5,3},{6,0},{7,5},{8,10},{9,15},{10,... | collective-permute-start | bytes 589832 | tf_op jit(solution)/shard_map/ppermute | solution.py:43
  11.2 3.2 %collective-permute-done.4.refs_1_ = bf16[64,3072]{1,0:T(8,128)(2,1)S(1)} collective-permute-done((bf16[64,3072]{1,0:T(8,128)(2,1)}, bf16[64,3072]{1,0:T(8,128)(2,1)S(1)}, u32[]{:S(2)}, u32[]{:S(2)}) %collective-permute-start.4) | collective-permute-done | bytes 393248 | tf_op jit(solution)/shard_map/ppermute | solution.py:48
  15.2 3.2 %front.3 = (bf16[36,3072]{1,0:T(8,128)(2,1)}, bf16[36,3072]{1,0:T(8,128)(2,1)}, bf16[36,3072]{1,0:T(8,128)(2,1)}, bf16[36,3072]{1,0:T(8,128)(2,1)}, bf16[32,3072...) custom-call(s32[2,2,2048]{2,1,0:T(2,128)} %bitcast.16, ...), custom_call_target="tpu_custom_call", output_to_operand_aliasing={{5}: (6, {})} | custom-call | flops 1024 | bytes 1024 | tf_op jit(solution)/shard_map/front/pallas_call | solution.py:124
  18.5 2.9 %collective-permute-done.2 = bf16[36,3072]{1,0:T(8,128)(2,1)S(1)} collective-permute-done((bf16[36,3072]{1,0:T(8,128)(2,1)}, bf16[36,3072]{1,0:T(8,128)(2,1)S(1)}, u32[]{:S(2)}, u32[]{:S(2)}) %collective-permute-start.2) | collective-permute-done | bytes 221216 | tf_op jit(solution)/shard_map/ppermute | solution.py:43
  23.9 1.5 %collective-permute-start.8 = (bf16[112,3072]{1,0:T(8,128)(2,1)S(1)}, bf16[112,3072]{1,0:T(8,128)(2,1)S(1)}, u32[]{:S(2)}, u32[]{:S(2)}) collective-permute-start(bf16[112,3072]{1,0:T(8,128)(2,1)S(1)} %slice.12), channel_id=1, source_target_pairs={{0,2},{1,7},{2,4},{3,1},{4,6},{5,3},{6,0},{7,5},{8,10},{9,15},{10,... | collective-permute-start | bytes 2064392 | tf_op jit(solution)/shard_map/ppermute | solution.py:43
  27.0 3.4 %plan.1 = (bf16[1152,864]{1,0:T(8,128)(2,1)S(1)}, bf16[1152,288]{1,0:T(8,128)(2,1)S(1)}, bf16[1152,864]{1,0:T(8,128)(2,1)S(1)}, bf16[1152,288]{1,0:T(8,128)(2,1)S(1)}) custom-call(s32[2,2,2048]{2,1,0:T(2,128)S(1)} %bitcast.17, s32[8,1152]{1,0:T(8,128)S(1)} %copy-done.2), custom_call_target="tpu_custom_call" | custom-call | flops 1024 | bytes 1024 | tf_op jit(solution)/shard_map/plan/pallas_call | solution.py:207
  30.4 1.8 %collective-permute-done.5 = bf16[36,3072]{1,0:T(8,128)(2,1)S(1)} collective-permute-done((bf16[36,3072]{1,0:T(8,128)(2,1)S(1)}, bf16[36,3072]{1,0:T(8,128)(2,1)S(1)}, u32[]{:S(2)}, u32[]{:S(2)}) %collective-permute-start.5) | collective-permute-done | bytes 221216 | tf_op jit(solution)/shard_map/ppermute | solution.py:43
  32.8 7.0 %collective-permute-done.7 = bf16[36,3072]{1,0:T(8,128)(2,1)S(1)} collective-permute-done((bf16[36,3072]{1,0:T(8,128)(2,1)S(1)}, bf16[36,3072]{1,0:T(8,128)(2,1)S(1)}, u32[]{:S(2)}, u32[]{:S(2)}) %collective-permute-start.7) | collective-permute-done | bytes 221216 | tf_op jit(solution)/shard_map/ppermute | solution.py:43
  41.8 2.3 %collective-permute-start.13 = (bf16[432,3072]{1,0:T(8,128)(2,1)S(1)}, bf16[432,3072]{1,0:T(8,128)(2,1)S(1)}, u32[]{:S(2)}, u32[]{:S(2)}) collective-permute-start(bf16[432,3072]{1,0:T(8,128)(2,1)S(1)} %pad_maximum_fusion), channel_id=1, source_target_pairs={{0,1},{1,0},{2,3},{3,2},{4,5},{5,4},{6,7},{7,6},{8,9},{9,8},{10,11... | collective-permute-start | bytes 7962632 | tf_op jit(solution)/shard_map/ppermute | solution.py:43
  45.2 1.9 %collective-permute-start.10 = (bf16[144,3072]{1,0:T(8,128)(2,1)S(1)}, bf16[144,3072]{1,0:T(8,128)(2,1)S(1)}, u32[]{:S(2)}, u32[]{:S(2)}) collective-permute-start(bf16[144,3072]{1,0:T(8,128)(2,1)S(1)} %pad_maximum_fusion.3.refs_0_), channel_id=1, source_target_pairs={{0,2},{1,7},{2,4},{3,1},{4,6},{5,3},{6,0},{7,5},{8,10},{9,15},{10,... | collective-permute-start | bytes 2654216 | tf_op jit(solution)/shard_map/ppermute | solution.py:43
  48.7 9.3 %near_product.2.near_ref = bf16[1152,1024]{1,0:T(8,128)(2,1)S(1)} custom-call(bf16[1152,864]{1,0:T(8,128)(2,1)S(1)} %get-tuple-element.81.placing_ref, bf16[1024,3072]{1,0:T(8,128)(2,1)S(1)} %bitcast.11, bf16[144,3072]{1,0:T(8,128)(2,1)S(1)} %pad_maximum_fusion.2.refs_0_, bf16[32,3072]{1,0:T(8,128)(2,1)S(1)} %collective-permute-done.3.refs_1_, ...), custom_call_target="tpu_custom_call" | custom-call | flops 1024 | bytes 1024 | tf_op jit(solution)/shard_map/near_product/pallas_call | solution.py:231
  58.0 5.2 %collective-permute-done.12.refs_0_ = bf16[144,3072]{1,0:T(8,128)(2,1)S(1)} collective-permute-done((bf16[144,3072]{1,0:T(8,128)(2,1)S(1)}, bf16[144,3072]{1,0:T(8,128)(2,1)S(1)}, u32[]{:S(2)}, u32[]{:S(2)}) %collective-permute-start.12) | collective-permute-done | bytes 884768 | tf_op jit(solution)/shard_map/ppermute | solution.py:43
  63.3 3.8 %collective-permute-start.14 = (bf16[80,3072]{1,0:T(8,128)(2,1)S(1)}, bf16[80,3072]{1,0:T(8,128)(2,1)S(1)}, u32[]{:S(2)}, u32[]{:S(2)}) collective-permute-start(bf16[80,3072]{1,0:T(8,128)(2,1)S(1)} %slice.10), channel_id=1, source_target_pairs={{0,1},{1,0},{2,3},{3,2},{4,5},{5,4},{6,7},{7,6},{8,9},{9,8},{10,11... | collective-permute-start | bytes 1474568 | tf_op jit(solution)/shard_map/ppermute | solution.py:43
  67.2 1.9 %collective-permute-done.15.refs_2_ = bf16[64,3072]{1,0:T(8,128)(2,1)S(1)} collective-permute-done((bf16[64,3072]{1,0:T(8,128)(2,1)S(1)}, bf16[64,3072]{1,0:T(8,128)(2,1)S(1)}, u32[]{:S(2)}, u32[]{:S(2)}) %collective-permute-start.15) | collective-permute-done | bytes 393248 | tf_op jit(solution)/shard_map/ppermute | solution.py:43
  69.2 4.2 %far_product.2.refs_2_ = bf16[2,1152,1024]{2,1,0:T(8,128)(2,1)} custom-call(bf16[1152,288]{1,0:T(8,128)(2,1)S(1)} %get-tuple-element.79.placing_ref, bf16[1024,3072]{1,0:T(8,128)(2,1)S(1)} %bitcast.12, bf16[1152,1024]{1,0:T(8,128)(2,1)S(1)} %near_product.2.near_ref, bf16[144,3072]{1,0:T(8,128)(2,1)S(1)} %collective-permute-done.12.refs_0_, ...), custom_call_target="tpu_custom_call" | custom-call | flops 1258291200 | bytes 1024 | tf_op jit(solution)/shard_map/far_product/pallas_call | solution.py:262
  73.3 2.9 %collective-permute-done.11.refs_2_ = bf16[144,3072]{1,0:T(8,128)(2,1)S(1)} collective-permute-done((bf16[144,3072]{1,0:T(8,128)(2,1)S(1)}, bf16[144,3072]{1,0:T(8,128)(2,1)S(1)}, u32[]{:S(2)}, u32[]{:S(2)}) %collective-permute-start.11) | collective-permute-done | bytes 884768 | tf_op jit(solution)/shard_map/ppermute | solution.py:43
  76.7 3.4 %collective-permute-start.16 = (bf16[144,3072]{1,0:T(8,128)(2,1)S(1)}, bf16[144,3072]{1,0:T(8,128)(2,1)S(1)}, u32[]{:S(2)}, u32[]{:S(2)}) collective-permute-start(bf16[144,3072]{1,0:T(8,128)(2,1)S(1)} %collective-permute-done.10.refs_1_), channel_id=1, source_target_pairs={{0,2},{1,7},{2,4},{3,1},{4,6},{5,3},{6,0},{7,5},{8,10},{9,15},{10,... | collective-permute-start | bytes 2654216 | tf_op jit(solution)/shard_map/ppermute | solution.py:43
  81.5 8.1 %near_product.3.near_ref = bf16[1152,1024]{1,0:T(8,128)(2,1)S(1)} custom-call(bf16[1152,864]{1,0:T(8,128)(2,1)S(1)} %get-tuple-element.88.placing_ref, bf16[1024,3072]{1,0:T(8,128)(2,1)S(1)} %bitcast.13, bf16[144,3072]{1,0:T(8,128)(2,1)S(1)} %pad_maximum_fusion.3.refs_0_, bf16[144,3072]{1,0:T(8,128)(2,1)S(1)} %collective-permute-done.10.refs_1_, ...), custom_call_target="tpu_custom_call" | custom-call | flops 1024 | bytes 1024 | tf_op jit(solution)/shard_map/near_product/pallas_call | solution.py:231
  90.1 1.6 %collective-permute-start.18 = (bf16[144,3072]{1,0:T(8,128)(2,1)S(1)}, bf16[144,3072]{1,0:T(8,128)(2,1)S(1)}, u32[]{:S(2)}, u32[]{:S(2)}) collective-permute-start(bf16[144,3072]{1,0:T(8,128)(2,1)S(1)} %collective-permute-done.16.refs_0_), channel_id=1, source_target_pairs={{0,1},{1,0},{2,3},{3,2},{4,5},{5,4},{6,7},{7,6},{8,9},{9,8},{10,11... | collective-permute-start | bytes 2654216 | tf_op jit(solution)/shard_map/ppermute | solution.py:43
  91.8 2.1 %collective-permute-done.18.refs_1_ = bf16[144,3072]{1,0:T(8,128)(2,1)S(1)} collective-permute-done((bf16[144,3072]{1,0:T(8,128)(2,1)S(1)}, bf16[144,3072]{1,0:T(8,128)(2,1)S(1)}, u32[]{:S(2)}, u32[]{:S(2)}) %collective-permute-start.18) | collective-permute-done | bytes 884768 | tf_op jit(solution)/shard_map/ppermute | solution.py:43
  93.8 4.2 %far_product.3 = bf16[2,1152,1024]{2,1,0:T(8,128)(2,1)} custom-call(bf16[1152,288]{1,0:T(8,128)(2,1)S(1)} %get-tuple-element.74.placing_ref, bf16[1024,3072]{1,0:T(8,128)(2,1)S(1)} %bitcast.14, bf16[1152,1024]{1,0:T(8,128)(2,1)S(1)} %near_product.3.near_ref, bf16[144,3072]{1,0:T(8,128)(2,1)S(1)} %collective-permute-done.16.refs_0_, ...), custom_call_target="tpu_custom_call", output_to_operand_aliasing={{}: (5, {})} | custom-call | flops 1258291200 | bytes 1024 | tf_op jit(solution)/shard_map/far_product/pallas_call | solution.py:262
  (44 shorter events, 12.6 us)
Async XLA Ops:
  3.7 10.7 %collective-permute-start.4 = (bf16[64,3072]{1,0:T(8,128)(2,1)}, bf16[64,3072]{1,0:T(8,128)(2,1)S(1)}, u32[]{:S(2)}, u32[]{:S(2)}) collective-permute-start(bf16[64,3072]{1,0:T(8,128)(2,1)} %get-tuple-element.53), channel_id=1, source_target_pairs={{32,0},{64,32},{96,64},{128,96},{160,128},{192,160},{224,192},{33,... | collective-permute-start | bytes 1179656 | tf_op jit(solution)/shard_map/ppermute | solution.py:48
  6.4 12.1 %collective-permute-start = (bf16[36,3072]{1,0:T(8,128)(2,1)}, bf16[36,3072]{1,0:T(8,128)(2,1)S(1)}, u32[]{:S(2)}, u32[]{:S(2)}) collective-permute-start(bf16[36,3072]{1,0:T(8,128)(2,1)} %get-tuple-element.49), channel_id=1, source_target_pairs={{0,8},{1,9},{2,10},{3,11},{4,12},{5,13},{6,14},{7,15},{8,16},{9,17... | collective-permute-start | bytes 663560 | tf_op jit(solution)/shard_map/ppermute | solution.py:43
  6.5 12.0 %collective-permute-start.1 = (bf16[36,3072]{1,0:T(8,128)(2,1)}, bf16[36,3072]{1,0:T(8,128)(2,1)S(1)}, u32[]{:S(2)}, u32[]{:S(2)}) collective-permute-start(bf16[36,3072]{1,0:T(8,128)(2,1)} %get-tuple-element.50), channel_id=1, source_target_pairs={{0,16},{1,17},{2,18},{3,19},{4,20},{5,21},{6,22},{7,23},{8,24},{9,... | collective-permute-start | bytes 663560 | tf_op jit(solution)/shard_map/ppermute | solution.py:43
  8.7 12.7 %collective-permute-start.2 = (bf16[36,3072]{1,0:T(8,128)(2,1)}, bf16[36,3072]{1,0:T(8,128)(2,1)S(1)}, u32[]{:S(2)}, u32[]{:S(2)}) collective-permute-start(bf16[36,3072]{1,0:T(8,128)(2,1)} %get-tuple-element.51), channel_id=1, source_target_pairs={{0,24},{1,25},{2,26},{3,27},{4,28},{5,29},{6,30},{7,31},{8,0},{9,1... | collective-permute-start | bytes 663560 | tf_op jit(solution)/shard_map/ppermute | solution.py:43
  8.7 9.7 %collective-permute-start.3 = (bf16[32,3072]{1,0:T(8,128)(2,1)}, bf16[32,3072]{1,0:T(8,128)(2,1)S(1)}, u32[]{:S(2)}, u32[]{:S(2)}) collective-permute-start(bf16[32,3072]{1,0:T(8,128)(2,1)} %get-tuple-element.52), channel_id=1, source_target_pairs={{0,2},{1,7},{2,4},{3,1},{4,6},{5,3},{6,0},{7,5},{8,10},{9,15},{10,... | collective-permute-start | bytes 589832 | tf_op jit(solution)/shard_map/ppermute | solution.py:43
  15.2 11.8 %copy-start.1 = (s32[1,2,2048,2]{2,3,1,0:T(2,128)S(1)}, s32[1,2,2048,2]{2,3,1,0:T(2,128)}, u32[]{:S(2)}) copy-start(s32[1,2,2048,2]{2,3,1,0:T(2,128)} %param.10) | copy-start | bytes 98308
  15.2 11.8 %copy-start.2 = (s32[8,1152]{1,0:T(8,128)S(1)}, s32[8,1152]{1,0:T(8,128)}, u32[]{:S(2)}) copy-start(s32[8,1152]{1,0:T(8,128)} %constant.2.clone.table_ref) | copy-start | bytes 110596
  18.4 7.9 %copy-start.5 = (bf16[36,3072]{1,0:T(8,128)(2,1)S(1)}, bf16[36,3072]{1,0:T(8,128)(2,1)}, u32[]{:S(2)}) copy-start(bf16[36,3072]{1,0:T(8,128)(2,1)} %get-tuple-element.64) | copy-start | bytes 663556
  22.5 19.0 %collective-permute-start.9 = (bf16[144,3072]{1,0:T(8,128)(2,1)S(1)}, bf16[144,3072]{1,0:T(8,128)(2,1)S(1)}, u32[]{:S(2)}, u32[]{:S(2)}) collective-permute-start(bf16[144,3072]{1,0:T(8,128)(2,1)S(1)} %pad_maximum_fusion.2.refs_0_), channel_id=1, source_target_pairs={{0,6},{1,3},{2,0},{3,5},{4,2},{5,7},{6,4},{7,1},{8,14},{9,11},{10,... | collective-permute-start | bytes 2654216 | tf_op jit(solution)/shard_map/ppermute | solution.py:43
  23.8 21.2 %copy-start.4 = (bf16[36,3072]{1,0:T(8,128)(2,1)S(1)}, bf16[36,3072]{1,0:T(8,128)(2,1)}, u32[]{:S(2)}) copy-start(bf16[36,3072]{1,0:T(8,128)(2,1)} %get-tuple-element.75) | copy-start | bytes 663556
  23.9 17.4 %collective-permute-start.8 = (bf16[112,3072]{1,0:T(8,128)(2,1)S(1)}, bf16[112,3072]{1,0:T(8,128)(2,1)S(1)}, u32[]{:S(2)}, u32[]{:S(2)}) collective-permute-start(bf16[112,3072]{1,0:T(8,128)(2,1)S(1)} %slice.12), channel_id=1, source_target_pairs={{0,2},{1,7},{2,4},{3,1},{4,6},{5,3},{6,0},{7,5},{8,10},{9,15},{10,... | collective-permute-start | bytes 2064392 | tf_op jit(solution)/shard_map/ppermute | solution.py:43
  25.4 6.8 %collective-permute-start.5 = (bf16[36,3072]{1,0:T(8,128)(2,1)S(1)}, bf16[36,3072]{1,0:T(8,128)(2,1)S(1)}, u32[]{:S(2)}, u32[]{:S(2)}) collective-permute-start(bf16[36,3072]{1,0:T(8,128)(2,1)S(1)} %copy-done.7), channel_id=1, source_target_pairs={{0,8},{1,9},{2,10},{3,11},{4,12},{5,13},{6,14},{7,15},{8,16},{9,17... | collective-permute-start | bytes 663560 | tf_op jit(solution)/shard_map/ppermute | solution.py:43
  25.4 7.4 %collective-permute-start.6 = (bf16[36,3072]{1,0:T(8,128)(2,1)S(1)}, bf16[36,3072]{1,0:T(8,128)(2,1)S(1)}, u32[]{:S(2)}, u32[]{:S(2)}) collective-permute-start(bf16[36,3072]{1,0:T(8,128)(2,1)S(1)} %copy-done.6), channel_id=1, source_target_pairs={{0,16},{1,17},{2,18},{3,19},{4,20},{5,21},{6,22},{7,23},{8,24},{9,... | collective-permute-start | bytes 663560 | tf_op jit(solution)/shard_map/ppermute | solution.py:43
  26.3 13.5 %collective-permute-start.7 = (bf16[36,3072]{1,0:T(8,128)(2,1)S(1)}, bf16[36,3072]{1,0:T(8,128)(2,1)S(1)}, u32[]{:S(2)}, u32[]{:S(2)}) collective-permute-start(bf16[36,3072]{1,0:T(8,128)(2,1)S(1)} %copy-done.5), channel_id=1, source_target_pairs={{0,24},{1,25},{2,26},{3,27},{4,28},{5,29},{6,30},{7,31},{8,0},{9,1... | collective-permute-start | bytes 663560 | tf_op jit(solution)/shard_map/ppermute | solution.py:43
  41.6 7.1 %copy-start = (bf16[1,1024,3072]{2,1,0:T(8,128)(2,1)S(1)}, bf16[1,1024,3072]{2,1,0:T(8,128)(2,1)}, u32[]{:S(2)}) copy-start(bf16[1,1024,3072]{2,1,0:T(8,128)(2,1)} %param.14) | copy-start | bytes 18874372
  41.8 6.9 %collective-permute-start.13 = (bf16[432,3072]{1,0:T(8,128)(2,1)S(1)}, bf16[432,3072]{1,0:T(8,128)(2,1)S(1)}, u32[]{:S(2)}, u32[]{:S(2)}) collective-permute-start(bf16[432,3072]{1,0:T(8,128)(2,1)S(1)} %pad_maximum_fusion), channel_id=1, source_target_pairs={{0,1},{1,0},{2,3},{3,2},{4,5},{5,4},{6,7},{7,6},{8,9},{9,8},{10,11... | collective-permute-start | bytes 7962632 | tf_op jit(solution)/shard_map/ppermute | solution.py:43
  44.1 19.2 %collective-permute-start.12 = (bf16[144,3072]{1,0:T(8,128)(2,1)S(1)}, bf16[144,3072]{1,0:T(8,128)(2,1)S(1)}, u32[]{:S(2)}, u32[]{:S(2)}) collective-permute-start(bf16[144,3072]{1,0:T(8,128)(2,1)S(1)} %collective-permute-done.9.refs_3_), channel_id=1, source_target_pairs={{0,6},{1,3},{2,0},{3,5},{4,2},{5,7},{6,4},{7,1},{8,14},{9,11},{10,... | collective-permute-start | bytes 2654216 | tf_op jit(solution)/shard_map/ppermute | solution.py:43
  45.2 28.1 %collective-permute-start.10 = (bf16[144,3072]{1,0:T(8,128)(2,1)S(1)}, bf16[144,3072]{1,0:T(8,128)(2,1)S(1)}, u32[]{:S(2)}, u32[]{:S(2)}) collective-permute-start(bf16[144,3072]{1,0:T(8,128)(2,1)S(1)} %pad_maximum_fusion.3.refs_0_), channel_id=1, source_target_pairs={{0,2},{1,7},{2,4},{3,1},{4,6},{5,3},{6,0},{7,5},{8,10},{9,15},{10,... | collective-permute-start | bytes 2654216 | tf_op jit(solution)/shard_map/ppermute | solution.py:43
  47.1 29.1 %collective-permute-start.11 = (bf16[144,3072]{1,0:T(8,128)(2,1)S(1)}, bf16[144,3072]{1,0:T(8,128)(2,1)S(1)}, u32[]{:S(2)}, u32[]{:S(2)}) collective-permute-start(bf16[144,3072]{1,0:T(8,128)(2,1)S(1)} %pad_maximum_fusion.3.refs_0_), channel_id=1, source_target_pairs={{0,6},{1,3},{2,0},{3,5},{4,2},{5,7},{6,4},{7,1},{8,14},{9,11},{10,... | collective-permute-start | bytes 2654216 | tf_op jit(solution)/shard_map/ppermute | solution.py:43
  63.3 5.9 %collective-permute-start.14 = (bf16[80,3072]{1,0:T(8,128)(2,1)S(1)}, bf16[80,3072]{1,0:T(8,128)(2,1)S(1)}, u32[]{:S(2)}, u32[]{:S(2)}) collective-permute-start(bf16[80,3072]{1,0:T(8,128)(2,1)S(1)} %slice.10), channel_id=1, source_target_pairs={{0,1},{1,0},{2,3},{3,2},{4,5},{5,4},{6,7},{7,6},{8,9},{9,8},{10,11... | collective-permute-start | bytes 1474568 | tf_op jit(solution)/shard_map/ppermute | solution.py:43
  67.1 2.0 %collective-permute-start.15 = (bf16[64,3072]{1,0:T(8,128)(2,1)S(1)}, bf16[64,3072]{1,0:T(8,128)(2,1)S(1)}, u32[]{:S(2)}, u32[]{:S(2)}) collective-permute-start(bf16[64,3072]{1,0:T(8,128)(2,1)S(1)} %slice.11), channel_id=1, source_target_pairs={{0,1},{1,0},{2,3},{3,2},{4,5},{5,4},{6,7},{7,6},{8,9},{9,8},{10,11... | collective-permute-start | bytes 1179656 | tf_op jit(solution)/shard_map/ppermute | solution.py:43
  76.4 5.0 %collective-permute-start.17 = (bf16[432,3072]{1,0:T(8,128)(2,1)S(1)}, bf16[432,3072]{1,0:T(8,128)(2,1)S(1)}, u32[]{:S(2)}, u32[]{:S(2)}) collective-permute-start(bf16[432,3072]{1,0:T(8,128)(2,1)S(1)} %pad_maximum_fusion.1), channel_id=1, source_target_pairs={{0,1},{1,0},{2,3},{3,2},{4,5},{5,4},{6,7},{7,6},{8,9},{9,8},{10,11... | collective-permute-start | bytes 7962632 | tf_op jit(solution)/shard_map/ppermute | solution.py:43
  76.7 13.4 %collective-permute-start.16 = (bf16[144,3072]{1,0:T(8,128)(2,1)S(1)}, bf16[144,3072]{1,0:T(8,128)(2,1)S(1)}, u32[]{:S(2)}, u32[]{:S(2)}) collective-permute-start(bf16[144,3072]{1,0:T(8,128)(2,1)S(1)} %collective-permute-done.10.refs_1_), channel_id=1, source_target_pairs={{0,2},{1,7},{2,4},{3,1},{4,6},{5,3},{6,0},{7,5},{8,10},{9,15},{10,... | collective-permute-start | bytes 2654216 | tf_op jit(solution)/shard_map/ppermute | solution.py:43
  90.1 3.7 %collective-permute-start.18 = (bf16[144,3072]{1,0:T(8,128)(2,1)S(1)}, bf16[144,3072]{1,0:T(8,128)(2,1)S(1)}, u32[]{:S(2)}, u32[]{:S(2)}) collective-permute-start(bf16[144,3072]{1,0:T(8,128)(2,1)S(1)} %collective-permute-done.16.refs_0_), channel_id=1, source_target_pairs={{0,1},{1,0},{2,3},{3,2},{4,5},{5,4},{6,7},{7,6},{8,9},{9,8},{10,11... | collective-permute-start | bytes 2654216 | tf_op jit(solution)/shard_map/ppermute | solution.py:43
  (3 other events, 14.7 us)
where the time goes:
time: 98.5 us; the launch traced here: 98.1 us
  Pallas kernels  35.5 us (36%)
  waiting for transfers between devices  32.9 us (33%)
  starting transfers between devices  26.3 us (27%)
  other arithmetic  1.64 us (2%)
  between operations  0.99 us (1%)
    ppermute x18, waiting for transfers between devices, hop(): return lax.ppermute(shard, 'ep', pairs)  29.6 us
    ppermute x18, starting transfers between devices, hop(): return lax.ppermute(shard, 'ep', pairs)  23.6 us
    pallas_call x2, Pallas kernels, near_product(): pl.pallas_call(functools.partial(near_kernel, len(pieces), unrolled), out...  17.4 us
    pallas_call x2, Pallas kernels, far_product(): pl.pallas_call(functools.partial(far_kernel, moment, len(pieces)), out_sh...  8.3 us
    pallas_call x2, Pallas kernels, front(): pl.pallas_call(functools.partial(front_kernel, moment, count), out_shape=...  6.3 us
    pallas_call x1, Pallas kernels, plan(): pl.pallas_call(plan_kernel, out_shape=[jax.ShapeDtypeStruct((MAXP, n), jn...  3.41 us
    ppermute x1, waiting for transfers between devices, down(): return lax.ppermute(shard, 'section', [(i, i - 1) for i in range(1, n)])  3.24 us
    ppermute x1, starting transfers between devices, down(): return lax.ppermute(shard, 'section', [(i, i - 1) for i in range(1, n)])  2.65 us
  transfers between devices with their start and end apart: 19, of which 14 were waited for; matrix products, arithmetic and copies ran while one was open for 0% of the time, Pallas kernels for 29%

commit v1 on v0

--- a/solution.py
+++ b/solution.py
@@ -20,6 +20,7 @@
 HEAD = 80
 DYS = (0, 1, 3, 2)
 GROUP = CORES * BLOCK
+PART = 112
 NEAR = 3 * GROUP
 OWN = 32
 STEP = 128
@@ -316,7 +317,8 @@
 
     far1 = hop(near1[1][0], dx=1)
     pieces = [block1, *near1[1], *near1[3]]
-    product1 = near_product(placing[2], [*pieces, swapped(jnp.concatenate(pieces))], down_rows, True)
+    chunks = [jnp.concatenate(pieces)[at : at + PART] for at in range(0, 3 * BLOCK, PART)]
+    product1 = near_product(placing[2], [*pieces, *swapped(chunks)], down_rows, True)
     far1, product1 = tie((far1, product1))
 
     hidden = far_product(1, placing[3], [far1, swapped(far1)], product1, down_rows, hidden)

time: 98.5 us -> 97.9 us (level)
  waiting for transfers between devices: 32.9 us -> 34.8 us
  starting transfers between devices: 26.3 us -> 24.5 us
    ppermute x18 -> x21, waiting for transfers between devices: 29.6 us -> 31.6 us  [hop(): return lax.ppermute(shard, 'ep', pairs)]
    ppermute x18 -> x21, starting transfers between devices: 23.6 us -> 21.7 us  [hop(): return lax.ppermute(shard, 'ep', pairs)]
  transfers between devices with their start and end apart: 19 -> 22, of which waited for: 14 -> 13; matrix products, arithmetic and copies ran while one was open for 0% -> 0% of each run, Pallas kernels for 29% -> 29%
where the time goes in v1:
time: 97.9 us; the launch traced here: 97.4 us
  Pallas kernels  35.4 us (36%)
  waiting for transfers between devices  34.8 us (36%)
  starting transfers between devices  24.5 us (25%)
  between operations  1.04 us (1%)
    ppermute x21, waiting for transfers between devices, hop(): return lax.ppermute(shard, 'ep', pairs)  31.6 us
    ppermute x21, starting transfers between devices, hop(): return lax.ppermute(shard, 'ep', pairs)  21.7 us
    pallas_call x2, Pallas kernels, near_product(): pl.pallas_call(functools.partial(near_kernel, len(pieces), unrolled), out...  17.5 us
    pallas_call x2, Pallas kernels, far_product(): pl.pallas_call(functools.partial(far_kernel, moment, len(pieces)), out_sh...  8.3 us
    pallas_call x2, Pallas kernels, front(): pl.pallas_call(functools.partial(front_kernel, moment, count), out_shape=...  6.28 us
    pallas_call x1, Pallas kernels, plan(): pl.pallas_call(plan_kernel, out_shape=[jax.ShapeDtypeStruct((MAXP, n), jn...  3.4 us
    ppermute x1, waiting for transfers between devices, down(): return lax.ppermute(shard, 'section', [(i, i - 1) for i in range(1, n)])  3.24 us
    ppermute x1, starting transfers between devices, down(): return lax.ppermute(shard, 'section', [(i, i - 1) for i in range(1, n)])  2.79 us
  transfers between devices with their start and end apart: 22, of which 13 were waited for; matrix products, arithmetic and copies ran while one was open for 0% of the time, Pallas kernels for 29%

profile of v1, /device:TPU:249, one launch (start us, length us, event | category | flops | bytes accessed | tf_op | source)
XLA Modules:
  0.0 97.4 jit_solution(17580210076872358653)
XLA Ops:
  0.6 3.1 %front.2 = (bf16[36,3072]{1,0:T(8,128)(2,1)}, bf16[36,3072]{1,0:T(8,128)(2,1)}, bf16[36,3072]{1,0:T(8,128)(2,1)}, bf16[36,3072]{1,0:T(8,128)(2,1)}, bf16[32,3072...) custom-call(s32[2,2,2048]{2,1,0:T(2,128)} %bitcast.15, f32[2,64]{1,0:T(2,128)} %bitcast.26, ...), custom_call_target="tpu_custom_call" | custom-call | flops 1024 | bytes 1024 | tf_op jit(solution)/shard_map/front/pallas_call | solution.py:125
  3.7 2.8 %collective-permute-start.4 = (bf16[64,3072]{1,0:T(8,128)(2,1)}, bf16[64,3072]{1,0:T(8,128)(2,1)S(1)}, u32[]{:S(2)}, u32[]{:S(2)}) collective-permute-start(bf16[64,3072]{1,0:T(8,128)(2,1)} %get-tuple-element.53), channel_id=1, source_target_pairs={{32,0},{64,32},{96,64},{128,96},{160,128},{192,160},{224,192},{33,... | collective-permute-start | bytes 1179656 | tf_op jit(solution)/shard_map/ppermute | solution.py:49
  6.6 2.2 %collective-permute-start.1 = (bf16[36,3072]{1,0:T(8,128)(2,1)}, bf16[36,3072]{1,0:T(8,128)(2,1)S(1)}, u32[]{:S(2)}, u32[]{:S(2)}) collective-permute-start(bf16[36,3072]{1,0:T(8,128)(2,1)} %get-tuple-element.50), channel_id=1, source_target_pairs={{0,16},{1,17},{2,18},{3,19},{4,20},{5,21},{6,22},{7,23},{8,24},{9,... | collective-permute-start | bytes 663560 | tf_op jit(solution)/shard_map/ppermute | solution.py:44
  8.9 2.5 %collective-permute-start.3 = (bf16[32,3072]{1,0:T(8,128)(2,1)}, bf16[32,3072]{1,0:T(8,128)(2,1)S(1)}, u32[]{:S(2)}, u32[]{:S(2)}) collective-permute-start(bf16[32,3072]{1,0:T(8,128)(2,1)} %get-tuple-element.52), channel_id=1, source_target_pairs={{0,2},{1,7},{2,4},{3,1},{4,6},{5,3},{6,0},{7,5},{8,10},{9,15},{10,... | collective-permute-start | bytes 589832 | tf_op jit(solution)/shard_map/ppermute | solution.py:44
  11.3 3.2 %collective-permute-done.4.refs_1_ = bf16[64,3072]{1,0:T(8,128)(2,1)S(1)} collective-permute-done((bf16[64,3072]{1,0:T(8,128)(2,1)}, bf16[64,3072]{1,0:T(8,128)(2,1)S(1)}, u32[]{:S(2)}, u32[]{:S(2)}) %collective-permute-start.4) | collective-permute-done | bytes 393248 | tf_op jit(solution)/shard_map/ppermute | solution.py:49
  15.3 3.2 %front.3 = (bf16[36,3072]{1,0:T(8,128)(2,1)}, bf16[36,3072]{1,0:T(8,128)(2,1)}, bf16[36,3072]{1,0:T(8,128)(2,1)}, bf16[36,3072]{1,0:T(8,128)(2,1)}, bf16[32,3072...) custom-call(s32[2,2,2048]{2,1,0:T(2,128)} %bitcast.16, ...), custom_call_target="tpu_custom_call", output_to_operand_aliasing={{5}: (6, {})} | custom-call | flops 1024 | bytes 1024 | tf_op jit(solution)/shard_map/front/pallas_call | solution.py:125
  18.6 2.9 %collective-permute-done.2 = bf16[36,3072]{1,0:T(8,128)(2,1)S(1)} collective-permute-done((bf16[36,3072]{1,0:T(8,128)(2,1)}, bf16[36,3072]{1,0:T(8,128)(2,1)S(1)}, u32[]{:S(2)}, u32[]{:S(2)}) %collective-permute-start.2) | collective-permute-done | bytes 221216 | tf_op jit(solution)/shard_map/ppermute | solution.py:44
  23.1 1.5 %collective-permute-start.8 = (bf16[112,3072]{1,0:T(8,128)(2,1)S(1)}, bf16[112,3072]{1,0:T(8,128)(2,1)S(1)}, u32[]{:S(2)}, u32[]{:S(2)}) collective-permute-start(bf16[112,3072]{1,0:T(8,128)(2,1)S(1)} %slice.28), channel_id=1, source_target_pairs={{0,2},{1,7},{2,4},{3,1},{4,6},{5,3},{6,0},{7,5},{8,10},{9,15},{10,... | collective-permute-start | bytes 2064392 | tf_op jit(solution)/shard_map/ppermute | solution.py:44
  26.2 3.4 %plan.1 = (bf16[1152,864]{1,0:T(8,128)(2,1)S(1)}, bf16[1152,288]{1,0:T(8,128)(2,1)S(1)}, bf16[1152,864]{1,0:T(8,128)(2,1)S(1)}, bf16[1152,288]{1,0:T(8,128)(2,1)S(1)}) custom-call(s32[2,2,2048]{2,1,0:T(2,128)S(1)} %bitcast.17, s32[8,1152]{1,0:T(8,128)S(1)} %copy-done.2), custom_call_target="tpu_custom_call" | custom-call | flops 1024 | bytes 1024 | tf_op jit(solution)/shard_map/plan/pallas_call | solution.py:208
  29.6 1.8 %collective-permute-done.5 = bf16[36,3072]{1,0:T(8,128)(2,1)S(1)} collective-permute-done((bf16[36,3072]{1,0:T(8,128)(2,1)S(1)}, bf16[36,3072]{1,0:T(8,128)(2,1)S(1)}, u32[]{:S(2)}, u32[]{:S(2)}) %collective-permute-start.5) | collective-permute-done | bytes 221216 | tf_op jit(solution)/shard_map/ppermute | solution.py:44
  32.0 7.0 %collective-permute-done.7 = bf16[36,3072]{1,0:T(8,128)(2,1)S(1)} collective-permute-done((bf16[36,3072]{1,0:T(8,128)(2,1)S(1)}, bf16[36,3072]{1,0:T(8,128)(2,1)S(1)}, u32[]{:S(2)}, u32[]{:S(2)}) %collective-permute-start.7) | collective-permute-done | bytes 221216 | tf_op jit(solution)/shard_map/ppermute | solution.py:44
  41.0 2.3 %collective-permute-start.13 = (bf16[432,3072]{1,0:T(8,128)(2,1)S(1)}, bf16[432,3072]{1,0:T(8,128)(2,1)S(1)}, u32[]{:S(2)}, u32[]{:S(2)}) collective-permute-start(bf16[432,3072]{1,0:T(8,128)(2,1)S(1)} %pad_maximum_fusion), channel_id=1, source_target_pairs={{0,1},{1,0},{2,3},{3,2},{4,5},{5,4},{6,7},{7,6},{8,9},{9,8},{10,11... | collective-permute-start | bytes 7962632 | tf_op jit(solution)/shard_map/ppermute | solution.py:44
  44.4 1.9 %collective-permute-start.10 = (bf16[144,3072]{1,0:T(8,128)(2,1)S(1)}, bf16[144,3072]{1,0:T(8,128)(2,1)S(1)}, u32[]{:S(2)}, u32[]{:S(2)}) collective-permute-start(bf16[144,3072]{1,0:T(8,128)(2,1)S(1)} %pad_maximum_fusion.2.refs_0_), channel_id=1, source_target_pairs={{0,2},{1,7},{2,4},{3,1},{4,6},{5,3},{6,0},{7,5},{8,10},{9,15},{10,... | collective-permute-start | bytes 2654216 | tf_op jit(solution)/shard_map/ppermute | solution.py:44
  47.8 9.4 %near_product.2.near_ref = bf16[1152,1024]{1,0:T(8,128)(2,1)S(1)} custom-call(bf16[1152,864]{1,0:T(8,128)(2,1)S(1)} %get-tuple-element.81.placing_ref, bf16[1024,3072]{1,0:T(8,128)(2,1)S(1)} %bitcast.11, bf16[144,3072]{1,0:T(8,128)(2,1)S(1)} %pad_maximum_fusion.1.refs_0_, bf16[32,3072]{1,0:T(8,128)(2,1)S(1)} %collective-permute-done.3.refs_1_, ...), custom_call_target="tpu_custom_call" | custom-call | flops 1024 | bytes 1024 | tf_op jit(solution)/shard_map/near_product/pallas_call | solution.py:232
  57.2 5.2 %collective-permute-done.12.refs_0_ = bf16[144,3072]{1,0:T(8,128)(2,1)S(1)} collective-permute-done((bf16[144,3072]{1,0:T(8,128)(2,1)S(1)}, bf16[144,3072]{1,0:T(8,128)(2,1)S(1)}, u32[]{:S(2)}, u32[]{:S(2)}) %collective-permute-start.12) | collective-permute-done | bytes 884768 | tf_op jit(solution)/shard_map/ppermute | solution.py:44
  62.5 3.8 %collective-permute-start.14 = (bf16[80,3072]{1,0:T(8,128)(2,1)S(1)}, bf16[80,3072]{1,0:T(8,128)(2,1)S(1)}, u32[]{:S(2)}, u32[]{:S(2)}) collective-permute-start(bf16[80,3072]{1,0:T(8,128)(2,1)S(1)} %slice.22), channel_id=1, source_target_pairs={{0,1},{1,0},{2,3},{3,2},{4,5},{5,4},{6,7},{7,6},{8,9},{9,8},{10,11... | collective-permute-start | bytes 1474568 | tf_op jit(solution)/shard_map/ppermute | solution.py:44
  66.4 1.9 %collective-permute-done.15.refs_2_ = bf16[64,3072]{1,0:T(8,128)(2,1)S(1)} collective-permute-done((bf16[64,3072]{1,0:T(8,128)(2,1)S(1)}, bf16[64,3072]{1,0:T(8,128)(2,1)S(1)}, u32[]{:S(2)}, u32[]{:S(2)}) %collective-permute-start.15) | collective-permute-done | bytes 393248 | tf_op jit(solution)/shard_map/ppermute | solution.py:44
  68.4 4.2 %far_product.2.refs_2_ = bf16[2,1152,1024]{2,1,0:T(8,128)(2,1)} custom-call(bf16[1152,288]{1,0:T(8,128)(2,1)S(1)} %get-tuple-element.79.placing_ref, bf16[1024,3072]{1,0:T(8,128)(2,1)S(1)} %bitcast.12, bf16[1152,1024]{1,0:T(8,128)(2,1)S(1)} %near_product.2.near_ref, bf16[144,3072]{1,0:T(8,128)(2,1)S(1)} %collective-permute-done.12.refs_0_, ...), custom_call_target="tpu_custom_call" | custom-call | flops 1258291200 | bytes 1024 | tf_op jit(solution)/shard_map/far_product/pallas_call | solution.py:263
  72.5 2.9 %collective-permute-done.11.refs_2_ = bf16[144,3072]{1,0:T(8,128)(2,1)S(1)} collective-permute-done((bf16[144,3072]{1,0:T(8,128)(2,1)S(1)}, bf16[144,3072]{1,0:T(8,128)(2,1)S(1)}, u32[]{:S(2)}, u32[]{:S(2)}) %collective-permute-start.11) | collective-permute-done | bytes 884768 | tf_op jit(solution)/shard_map/ppermute | solution.py:44
  75.5 1.8 %collective-permute-start.16 = (bf16[144,3072]{1,0:T(8,128)(2,1)S(1)}, bf16[144,3072]{1,0:T(8,128)(2,1)S(1)}, u32[]{:S(2)}, u32[]{:S(2)}) collective-permute-start(bf16[144,3072]{1,0:T(8,128)(2,1)S(1)} %collective-permute-done.10.refs_1_), channel_id=1, source_target_pairs={{0,2},{1,7},{2,4},{3,1},{4,6},{5,3},{6,0},{7,5},{8,10},{9,15},{10,... | collective-permute-start | bytes 2654216 | tf_op jit(solution)/shard_map/ppermute | solution.py:44
  78.8 3.6 %collective-permute-done.20.refs_6_ = bf16[96,3072]{1,0:T(8,128)(2,1)S(1)} collective-permute-done((bf16[96,3072]{1,0:T(8,128)(2,1)S(1)}, bf16[96,3072]{1,0:T(8,128)(2,1)S(1)}, u32[]{:S(2)}, u32[]{:S(2)}) %collective-permute-start.20) | collective-permute-done | bytes 589856 | tf_op jit(solution)/shard_map/ppermute | solution.py:44
  82.4 8.1 %near_product.3.near_ref = bf16[1152,1024]{1,0:T(8,128)(2,1)S(1)} custom-call(bf16[1152,864]{1,0:T(8,128)(2,1)S(1)} %get-tuple-element.88.placing_ref, bf16[1024,3072]{1,0:T(8,128)(2,1)S(1)} %bitcast.13, bf16[144,3072]{1,0:T(8,128)(2,1)S(1)} %pad_maximum_fusion.2.refs_0_, bf16[144,3072]{1,0:T(8,128)(2,1)S(1)} %collective-permute-done.10.refs_1_, ...), custom_call_target="tpu_custom_call" | custom-call | flops 1024 | bytes 1024 | tf_op jit(solution)/shard_map/near_product/pallas_call | solution.py:232
  90.7 2.3 %collective-permute-done.21.refs_1_ = bf16[144,3072]{1,0:T(8,128)(2,1)S(1)} collective-permute-done((bf16[144,3072]{1,0:T(8,128)(2,1)S(1)}, bf16[144,3072]{1,0:T(8,128)(2,1)S(1)}, u32[]{:S(2)}, u32[]{:S(2)}) %collective-permute-start.21) | collective-permute-done | bytes 884768 | tf_op jit(solution)/shard_map/ppermute | solution.py:44
  93.0 4.2 %far_product.3 = bf16[2,1152,1024]{2,1,0:T(8,128)(2,1)} custom-call(bf16[1152,288]{1,0:T(8,128)(2,1)S(1)} %get-tuple-element.74.placing_ref, bf16[1024,3072]{1,0:T(8,128)(2,1)S(1)} %bitcast.14, bf16[1152,1024]{1,0:T(8,128)(2,1)S(1)} %near_product.3.near_ref, bf16[144,3072]{1,0:T(8,128)(2,1)S(1)} %collective-permute-done.16.refs_0_, ...), custom_call_target="tpu_custom_call", output_to_operand_aliasing={{}: (5, {})} | custom-call | flops 1258291200 | bytes 1024 | tf_op jit(solution)/shard_map/far_product/pallas_call | solution.py:263
  (53 shorter events, 11.2 us)
Async XLA Ops:
  3.7 17.8 %copy-start.5 = (bf16[36,3072]{1,0:T(8,128)(2,1)S(1)}, bf16[36,3072]{1,0:T(8,128)(2,1)}, u32[]{:S(2)}) copy-start(bf16[36,3072]{1,0:T(8,128)(2,1)} %get-tuple-element.65) | copy-start | bytes 663556
  3.7 10.8 %collective-permute-start.4 = (bf16[64,3072]{1,0:T(8,128)(2,1)}, bf16[64,3072]{1,0:T(8,128)(2,1)S(1)}, u32[]{:S(2)}, u32[]{:S(2)}) collective-permute-start(bf16[64,3072]{1,0:T(8,128)(2,1)} %get-tuple-element.53), channel_id=1, source_target_pairs={{32,0},{64,32},{96,64},{128,96},{160,128},{192,160},{224,192},{33,... | collective-permute-start | bytes 1179656 | tf_op jit(solution)/shard_map/ppermute | solution.py:49
  6.5 12.1 %collective-permute-start = (bf16[36,3072]{1,0:T(8,128)(2,1)}, bf16[36,3072]{1,0:T(8,128)(2,1)S(1)}, u32[]{:S(2)}, u32[]{:S(2)}) collective-permute-start(bf16[36,3072]{1,0:T(8,128)(2,1)} %get-tuple-element.49), channel_id=1, source_target_pairs={{0,8},{1,9},{2,10},{3,11},{4,12},{5,13},{6,14},{7,15},{8,16},{9,17... | collective-permute-start | bytes 663560 | tf_op jit(solution)/shard_map/ppermute | solution.py:44
  6.6 12.0 %collective-permute-start.1 = (bf16[36,3072]{1,0:T(8,128)(2,1)}, bf16[36,3072]{1,0:T(8,128)(2,1)S(1)}, u32[]{:S(2)}, u32[]{:S(2)}) collective-permute-start(bf16[36,3072]{1,0:T(8,128)(2,1)} %get-tuple-element.50), channel_id=1, source_target_pairs={{0,16},{1,17},{2,18},{3,19},{4,20},{5,21},{6,22},{7,23},{8,24},{9,... | collective-permute-start | bytes 663560 | tf_op jit(solution)/shard_map/ppermute | solution.py:44
  8.9 12.7 %collective-permute-start.2 = (bf16[36,3072]{1,0:T(8,128)(2,1)}, bf16[36,3072]{1,0:T(8,128)(2,1)S(1)}, u32[]{:S(2)}, u32[]{:S(2)}) collective-permute-start(bf16[36,3072]{1,0:T(8,128)(2,1)} %get-tuple-element.51), channel_id=1, source_target_pairs={{0,24},{1,25},{2,26},{3,27},{4,28},{5,29},{6,30},{7,31},{8,0},{9,1... | collective-permute-start | bytes 663560 | tf_op jit(solution)/shard_map/ppermute | solution.py:44
  8.9 9.7 %collective-permute-start.3 = (bf16[32,3072]{1,0:T(8,128)(2,1)}, bf16[32,3072]{1,0:T(8,128)(2,1)S(1)}, u32[]{:S(2)}, u32[]{:S(2)}) collective-permute-start(bf16[32,3072]{1,0:T(8,128)(2,1)} %get-tuple-element.52), channel_id=1, source_target_pairs={{0,2},{1,7},{2,4},{3,1},{4,6},{5,3},{6,0},{7,5},{8,10},{9,15},{10,... | collective-permute-start | bytes 589832 | tf_op jit(solution)/shard_map/ppermute | solution.py:44
  21.7 19.0 %collective-permute-start.9 = (bf16[144,3072]{1,0:T(8,128)(2,1)S(1)}, bf16[144,3072]{1,0:T(8,128)(2,1)S(1)}, u32[]{:S(2)}, u32[]{:S(2)}) collective-permute-start(bf16[144,3072]{1,0:T(8,128)(2,1)S(1)} %pad_maximum_fusion.1.refs_0_), channel_id=1, source_target_pairs={{0,6},{1,3},{2,0},{3,5},{4,2},{5,7},{6,4},{7,1},{8,14},{9,11},{10,... | collective-permute-start | bytes 2654216 | tf_op jit(solution)/shard_map/ppermute | solution.py:44
  23.0 21.2 %copy-start.4 = (bf16[36,3072]{1,0:T(8,128)(2,1)S(1)}, bf16[36,3072]{1,0:T(8,128)(2,1)}, u32[]{:S(2)}) copy-start(bf16[36,3072]{1,0:T(8,128)(2,1)} %get-tuple-element.75) | copy-start | bytes 663556
  23.1 17.4 %collective-permute-start.8 = (bf16[112,3072]{1,0:T(8,128)(2,1)S(1)}, bf16[112,3072]{1,0:T(8,128)(2,1)S(1)}, u32[]{:S(2)}, u32[]{:S(2)}) collective-permute-start(bf16[112,3072]{1,0:T(8,128)(2,1)S(1)} %slice.28), channel_id=1, source_target_pairs={{0,2},{1,7},{2,4},{3,1},{4,6},{5,3},{6,0},{7,5},{8,10},{9,15},{10,... | collective-permute-start | bytes 2064392 | tf_op jit(solution)/shard_map/ppermute | solution.py:44
  24.6 6.8 %collective-permute-start.5 = (bf16[36,3072]{1,0:T(8,128)(2,1)S(1)}, bf16[36,3072]{1,0:T(8,128)(2,1)S(1)}, u32[]{:S(2)}, u32[]{:S(2)}) collective-permute-start(bf16[36,3072]{1,0:T(8,128)(2,1)S(1)} %copy-done.8), channel_id=1, source_target_pairs={{0,8},{1,9},{2,10},{3,11},{4,12},{5,13},{6,14},{7,15},{8,16},{9,17... | collective-permute-start | bytes 663560 | tf_op jit(solution)/shard_map/ppermute | solution.py:44
  24.6 7.4 %collective-permute-start.6 = (bf16[36,3072]{1,0:T(8,128)(2,1)S(1)}, bf16[36,3072]{1,0:T(8,128)(2,1)S(1)}, u32[]{:S(2)}, u32[]{:S(2)}) collective-permute-start(bf16[36,3072]{1,0:T(8,128)(2,1)S(1)} %copy-done.7), channel_id=1, source_target_pairs={{0,16},{1,17},{2,18},{3,19},{4,20},{5,21},{6,22},{7,23},{8,24},{9,... | collective-permute-start | bytes 663560 | tf_op jit(solution)/shard_map/ppermute | solution.py:44
  25.5 13.5 %collective-permute-start.7 = (bf16[36,3072]{1,0:T(8,128)(2,1)S(1)}, bf16[36,3072]{1,0:T(8,128)(2,1)S(1)}, u32[]{:S(2)}, u32[]{:S(2)}) collective-permute-start(bf16[36,3072]{1,0:T(8,128)(2,1)S(1)} %copy-done.6), channel_id=1, source_target_pairs={{0,24},{1,25},{2,26},{3,27},{4,28},{5,29},{6,30},{7,31},{8,0},{9,1... | collective-permute-start | bytes 663560 | tf_op jit(solution)/shard_map/ppermute | solution.py:44
  41.0 6.9 %collective-permute-start.13 = (bf16[432,3072]{1,0:T(8,128)(2,1)S(1)}, bf16[432,3072]{1,0:T(8,128)(2,1)S(1)}, u32[]{:S(2)}, u32[]{:S(2)}) collective-permute-start(bf16[432,3072]{1,0:T(8,128)(2,1)S(1)} %pad_maximum_fusion), channel_id=1, source_target_pairs={{0,1},{1,0},{2,3},{3,2},{4,5},{5,4},{6,7},{7,6},{8,9},{9,8},{10,11... | collective-permute-start | bytes 7962632 | tf_op jit(solution)/shard_map/ppermute | solution.py:44
  43.3 19.2 %collective-permute-start.12 = (bf16[144,3072]{1,0:T(8,128)(2,1)S(1)}, bf16[144,3072]{1,0:T(8,128)(2,1)S(1)}, u32[]{:S(2)}, u32[]{:S(2)}) collective-permute-start(bf16[144,3072]{1,0:T(8,128)(2,1)S(1)} %collective-permute-done.9.refs_3_), channel_id=1, source_target_pairs={{0,6},{1,3},{2,0},{3,5},{4,2},{5,7},{6,4},{7,1},{8,14},{9,11},{10,... | collective-permute-start | bytes 2654216 | tf_op jit(solution)/shard_map/ppermute | solution.py:44
  44.4 28.1 %collective-permute-start.10 = (bf16[144,3072]{1,0:T(8,128)(2,1)S(1)}, bf16[144,3072]{1,0:T(8,128)(2,1)S(1)}, u32[]{:S(2)}, u32[]{:S(2)}) collective-permute-start(bf16[144,3072]{1,0:T(8,128)(2,1)S(1)} %pad_maximum_fusion.2.refs_0_), channel_id=1, source_target_pairs={{0,2},{1,7},{2,4},{3,1},{4,6},{5,3},{6,0},{7,5},{8,10},{9,15},{10,... | collective-permute-start | bytes 2654216 | tf_op jit(solution)/shard_map/ppermute | solution.py:44
  46.3 29.1 %collective-permute-start.11 = (bf16[144,3072]{1,0:T(8,128)(2,1)S(1)}, bf16[144,3072]{1,0:T(8,128)(2,1)S(1)}, u32[]{:S(2)}, u32[]{:S(2)}) collective-permute-start(bf16[144,3072]{1,0:T(8,128)(2,1)S(1)} %pad_maximum_fusion.2.refs_0_), channel_id=1, source_target_pairs={{0,6},{1,3},{2,0},{3,5},{4,2},{5,7},{6,4},{7,1},{8,14},{9,11},{10,... | collective-permute-start | bytes 2654216 | tf_op jit(solution)/shard_map/ppermute | solution.py:44
  62.5 5.9 %collective-permute-start.14 = (bf16[80,3072]{1,0:T(8,128)(2,1)S(1)}, bf16[80,3072]{1,0:T(8,128)(2,1)S(1)}, u32[]{:S(2)}, u32[]{:S(2)}) collective-permute-start(bf16[80,3072]{1,0:T(8,128)(2,1)S(1)} %slice.22), channel_id=1, source_target_pairs={{0,1},{1,0},{2,3},{3,2},{4,5},{5,4},{6,7},{7,6},{8,9},{9,8},{10,11... | collective-permute-start | bytes 1474568 | tf_op jit(solution)/shard_map/ppermute | solution.py:44
  66.3 2.0 %collective-permute-start.15 = (bf16[64,3072]{1,0:T(8,128)(2,1)S(1)}, bf16[64,3072]{1,0:T(8,128)(2,1)S(1)}, u32[]{:S(2)}, u32[]{:S(2)}) collective-permute-start(bf16[64,3072]{1,0:T(8,128)(2,1)S(1)} %slice.23), channel_id=1, source_target_pairs={{0,1},{1,0},{2,3},{3,2},{4,5},{5,4},{6,7},{7,6},{8,9},{9,8},{10,11... | collective-permute-start | bytes 1179656 | tf_op jit(solution)/shard_map/ppermute | solution.py:44
  75.5 15.1 %collective-permute-start.16 = (bf16[144,3072]{1,0:T(8,128)(2,1)S(1)}, bf16[144,3072]{1,0:T(8,128)(2,1)S(1)}, u32[]{:S(2)}, u32[]{:S(2)}) collective-permute-start(bf16[144,3072]{1,0:T(8,128)(2,1)S(1)} %collective-permute-done.10.refs_1_), channel_id=1, source_target_pairs={{0,2},{1,7},{2,4},{3,1},{4,6},{5,3},{6,0},{7,5},{8,10},{9,15},{10,... | collective-permute-start | bytes 2654216 | tf_op jit(solution)/shard_map/ppermute | solution.py:44
  77.3 5.0 %collective-permute-start.17 = (bf16[112,3072]{1,0:T(8,128)(2,1)S(1)}, bf16[112,3072]{1,0:T(8,128)(2,1)S(1)}, u32[]{:S(2)}, u32[]{:S(2)}) collective-permute-start(bf16[112,3072]{1,0:T(8,128)(2,1)S(1)} %get-tuple-element.96), channel_id=1, source_target_pairs={{0,1},{1,0},{2,3},{3,2},{4,5},{5,4},{6,7},{7,6},{8,9},{9,8},{10,11... | collective-permute-start | bytes 2064392 | tf_op jit(solution)/shard_map/ppermute | solution.py:44
  77.4 4.9 %collective-permute-start.18 = (bf16[112,3072]{1,0:T(8,128)(2,1)S(1)}, bf16[112,3072]{1,0:T(8,128)(2,1)S(1)}, u32[]{:S(2)}, u32[]{:S(2)}) collective-permute-start(bf16[112,3072]{1,0:T(8,128)(2,1)S(1)} %get-tuple-element.95), channel_id=1, source_target_pairs={{0,1},{1,0},{2,3},{3,2},{4,5},{5,4},{6,7},{7,6},{8,9},{9,8},{10,11... | collective-permute-start | bytes 2064392 | tf_op jit(solution)/shard_map/ppermute | solution.py:44
  77.9 4.5 %collective-permute-start.19 = (bf16[112,3072]{1,0:T(8,128)(2,1)S(1)}, bf16[112,3072]{1,0:T(8,128)(2,1)S(1)}, u32[]{:S(2)}, u32[]{:S(2)}) collective-permute-start(bf16[112,3072]{1,0:T(8,128)(2,1)S(1)} %get-tuple-element.94), channel_id=1, source_target_pairs={{0,1},{1,0},{2,3},{3,2},{4,5},{5,4},{6,7},{7,6},{8,9},{9,8},{10,11... | collective-permute-start | bytes 2064392 | tf_op jit(solution)/shard_map/ppermute | solution.py:44
  78.1 4.3 %collective-permute-start.20 = (bf16[96,3072]{1,0:T(8,128)(2,1)S(1)}, bf16[96,3072]{1,0:T(8,128)(2,1)S(1)}, u32[]{:S(2)}, u32[]{:S(2)}) collective-permute-start(bf16[96,3072]{1,0:T(8,128)(2,1)S(1)} %slice.27), channel_id=1, source_target_pairs={{0,1},{1,0},{2,3},{3,2},{4,5},{5,4},{6,7},{7,6},{8,9},{9,8},{10,11... | collective-permute-start | bytes 1769480 | tf_op jit(solution)/shard_map/ppermute | solution.py:44
  90.5 2.5 %collective-permute-start.21 = (bf16[144,3072]{1,0:T(8,128)(2,1)S(1)}, bf16[144,3072]{1,0:T(8,128)(2,1)S(1)}, u32[]{:S(2)}, u32[]{:S(2)}) collective-permute-start(bf16[144,3072]{1,0:T(8,128)(2,1)S(1)} %collective-permute-done.16.refs_0_), channel_id=1, source_target_pairs={{0,1},{1,0},{2,3},{3,2},{4,5},{5,4},{6,7},{7,6},{8,9},{9,8},{10,11... | collective-permute-start | bytes 2654216 | tf_op jit(solution)/shard_map/ppermute | solution.py:44
  (7 other events, 42.2 us)
